TPU v7x, 256 devices: a whole 4x4x8 slice. The times are simulated.
256 devices in a mesh: dp: 8 (over y, core), vocab: 32 (over x, z).
Axes of the slice: x: 4, y: 4, z: 8, core: 2. Of those that a mesh axis runs over, the one named last changes fastest.
Arguments:
- grads: bfloat16 [8, 8192, 4608], P('dp', 'vocab'), may hold values from -6 to 6
- errors: bfloat16 [8, 8192, 4608], P('dp', 'vocab'), may hold values from -4 to 4
- start_q: float32 [4608, 32], replicated, may hold values from -6 to 6
Outputs:
- right_factor: float32 [4608, 32], replicated
- new_errors: bfloat16 [8, 8192, 4608], P('dp', 'vocab')
All inputs are finite; a program needn't handle non-finite values.
Results may differ from a plain program's by a relative error of at most 0.001.
Values sent between devices are 32-bit elements; how exact they have to be, the bound alone decides.
A program may use at most 64 MiB of HBM per device.

v0:
```python
import jax
import jax.numpy as jnp
from jax import lax
from jax.sharding import PartitionSpec as P

ITERS = 2


def body(grads, errors, start_q):
    hi = lax.Precision.HIGHEST
    replicas = lax.axis_size("dp")
    mixed = grads[0].astype(jnp.float32) + errors[0].astype(jnp.float32)
    q_now = start_q
    basis = None
    for step in range(ITERS):
        left = lax.psum(jnp.dot(mixed, q_now, precision=hi), "dp")
        gram = lax.psum(jnp.dot(left.T, left, precision=hi), "vocab")
        lower = jnp.linalg.cholesky(gram)
        basis = lax.linalg.triangular_solve(
            lower, left, left_side=False, lower=True, transpose_a=True
        )
        q_now = lax.psum(jnp.dot(mixed.T, basis, precision=hi), ("dp", "vocab")) / replicas
    approx = jnp.dot(basis, q_now.T, precision=hi)
    new_errors = (mixed - approx).astype(jnp.bfloat16)[None]
    return (q_now, new_errors)


def solution(mesh):
    return jax.shard_map(
        body,
        mesh=mesh,
        in_specs=(P("dp", "vocab", None), P("dp", "vocab", None), P()),
        out_specs=(P(), P("dp", "vocab", None)),
        check_vma=False,
    )
```

profile of v0, /device:TPU:1, one launch (start us, length us, event | category | flops | bytes accessed | tf_op | source)
XLA Modules:
  0.0 881.8 jit_solution(4473347561421761833)
XLA Ops:
  7.2 0.0 copy-start
  7.2 0.0 copy-start.1
  7.2 0.0 all-reduce.3.cloned.1.call-start
  7.2 1.0 copy-done
  8.2 6.6 fusion.8
  14.8 23.8 %psum.42 = f32[256,32]{0,1:T(8,128)S(1)} all-reduce(f32[256,32]{0,1:T(8,128)S(1)} %fusion.8), channel_id=1, replica_groups=mesh['dp'=8,'vocab'=32] {'dp'}, use_global_device_ids=true, to_apply=%region_0.0 | all-reduce | flops 8192 | bytes 65536 | tf_op jit(solution)/shard_map/psum | solution.py:16
  38.7 0.2 fusion.21
  38.8 118.1 %psum.43 = f32[32,32]{0,1:T(8,128)S(1)} all-reduce(f32[32,32]{0,1:T(8,128)S(1)} %fusion.21), channel_id=1, replica_groups=mesh['dp'=8,'vocab'=32] {'vocab'}, use_global_device_ids=true, to_apply=%region_1.0 | all-reduce | flops 1024 | bytes 8192 | tf_op jit(solution)/shard_map/psum | solution.py:17
  156.9 0.1 copy.6
  157.0 2.9 cholesky.44
  160.0 0.6 compare_reduce_fusion.1
  160.6 0.7 fusion.12
  161.3 2.4 custom-call.6
  163.7 0.2 convolution_bitcast_fusion.1
  164.0 0.0 copy-done.1
  164.0 5.8 fusion.6
  169.8 0.0 all-reduce.3.cloned.1.call-update
  169.8 0.0 all-reduce.5.cloned.1.call-start
  169.9 271.1 %all-reduce.3.cloned.1.call-done = f32[4608,32]{0,1:T(8,128)} async-done(((f32[4608,32]{0,1:T(8,128)}), f32[4608,32]{0,1:T(8,128)}) %all-reduce.3.cloned.1.call-update) | async-done | bytes 589840 | tf_op jit(solution)/shard_map/psum | solution.py:22
  441.0 6.0 fusion.4
  447.0 22.7 %psum.45 = f32[256,32]{0,1:T(8,128)S(1)} all-reduce(f32[256,32]{0,1:T(8,128)S(1)} %fusion.4), channel_id=1, replica_groups=mesh['dp'=8,'vocab'=32] {'dp'}, use_global_device_ids=true, to_apply=%region_5.8 | all-reduce | flops 8192 | bytes 65536 | tf_op jit(solution)/shard_map/psum | solution.py:16
  469.8 0.2 fusion.22
  469.9 113.1 %psum.46 = f32[32,32]{0,1:T(8,128)S(1)} all-reduce(f32[32,32]{0,1:T(8,128)S(1)} %fusion.22), channel_id=1, replica_groups=mesh['dp'=8,'vocab'=32] {'vocab'}, use_global_device_ids=true, to_apply=%region_6.9 | all-reduce | flops 1024 | bytes 8192 | tf_op jit(solution)/shard_map/psum | solution.py:17
  583.0 0.1 copy.8
  583.1 2.9 cholesky.55
  586.1 0.6 compare_reduce_fusion
  586.7 0.7 fusion.13
  587.4 2.4 custom-call.7
  589.8 0.2 convolution_bitcast_fusion
  590.1 5.8 fusion.2
  595.9 0.0 all-reduce.5.cloned.1.call-update
  595.9 271.1 %all-reduce.5.cloned.1.call-done = f32[4608,32]{0,1:T(8,128)} async-done(((f32[4608,32]{0,1:T(8,128)}), f32[4608,32]{0,1:T(8,128)}) %all-reduce.5.cloned.1.call-update) | async-done | bytes 589840 | tf_op jit(solution)/shard_map/psum | solution.py:22
  867.0 1.1 broadcast_multiply_fusion
  868.2 0.0 copy-start.2
  868.2 6.8 fusion.1
  875.0 0.0 copy-done.2
  (4 shorter events, 0.1 us)
Async XLA Ops:
  7.2 1.1 copy-start
  7.2 156.8 %copy-start.1 = (bf16[1,256,4608]{2,1,0:T(8,128)(2,1)S(1)}, bf16[1,256,4608]{2,1,0:T(8,128)(2,1)}, u32[]{:S(2)}) copy-start(bf16[1,256,4608]{2,1,0:T(8,128)(2,1)} %param.7) | copy-start | bytes 7077892
  7.2 433.8 %all-reduce.3.cloned.1.call-start = ((), (), s32[]{:S(2)}) async-start(), calls=%async_computation | async-start | bytes 1179648 | tf_op jit(solution)/shard_map/psum | solution.py:22
  169.8 697.2 %all-reduce.5.cloned.1.call-start = ((), (), s32[]{:S(2)}) async-start(), calls=%async_computation.1 | async-start | bytes 1179648 | tf_op jit(solution)/shard_map/psum | solution.py:22
  868.2 6.8 copy-start.2
Sparse Core Ops, SparseCore 0:
  170.0 270.9 all-reduce.2
  596.0 270.9 all-reduce.4
where the time goes:
time: 882 us
  waiting for transfers between devices  542 us (61%)
  blocking collectives  278 us (32%)
  matrix products  31.9 us (4%)
  other arithmetic  14.5 us (2%)
  between operations  14.1 us (2%)
    psum x2, waiting for transfers between devices, body(): lax.psum(jnp.dot(mixed.T, basis, precision=hi), ('dp', 'vocab')) / replicas  542 us
    psum x2, blocking collectives, body(): gram = lax.psum(jnp.dot(left.T, left, precision=hi), 'vocab')  231 us
    psum x2, blocking collectives, body(): left = lax.psum(jnp.dot(mixed, q_now, precision=hi), 'dp')  46.6 us
  transfers between devices with their start and end apart: 2, of which 2 were waited for; matrix products, arithmetic and copies ran while one was open for 0% of the time, Pallas kernels for 0%

commit v1 on v0

v1 whole, which is shorter than its diff:
```python
import functools

import jax
import jax.numpy as jnp
from jax import lax
from jax.experimental import pallas as pl
from jax.experimental.pallas import tpu as pltpu
from jax.sharding import PartitionSpec as P

MESH = pl.DeviceIdType.MESH
F32, BF16 = jnp.float32, jnp.bfloat16
ITERS = 2
RANK = 32
LANES = 128
STEP = 768
WINDOW = 5
Y, X, Z = 4, 4, 8
PLANE = Y * X


def split(value):
    high = value.astype(BF16)
    rest = value - high.astype(F32)
    middle = rest.astype(BF16)
    return high, middle, (rest - middle.astype(F32)).astype(BF16)


def dot(a, b, over_a, over_b):
    return lax.dot_general(a, b, (((over_a,), (over_b,)), ((), ())), preferred_element_type=F32)


def lower_inverse(packed):
    row = lax.broadcasted_iota(jnp.int32, (RANK, LANES), 0)
    lane = lax.broadcasted_iota(jnp.int32, (RANK, LANES), 1)
    turned = [packed if r == 1 else pltpu.roll(packed, (RANK - RANK * r) % LANES, 1) for r in range(4)]
    work = jnp.where(lane < RANK, jnp.where(lane == row, 1.0, 0.0), jnp.concatenate(turned, axis=0))
    rows = row[:, :1]
    pivots = jnp.ones((RANK, 1), F32)
    for j in range(RANK):
        column, pivot = work[:, RANK + j : RANK + j + 1], work[j : j + 1, RANK + j : RANK + j + 1]
        factor = jnp.where(rows > j, column / pivot, 0.0)
        pivots = jnp.where(rows == j, pivot, pivots)
        work = work - factor * work[j : j + 1, :]
    return (work * lax.rsqrt(pivots))[:, :RANK]


def six(value):
    high, middle, low = split(value)
    return jnp.concatenate([high, high, high, middle, middle, low], axis=1)


def six_rows(value):
    high, middle, low = split(value)
    return jnp.concatenate([high, middle, low, high, middle, high], axis=0)


def kernel(
    g_hbm, e_hbm, q_ref, rf_hbm, o_hbm,
    g, e, o, rf, lp, lr, ly, gx, u, pr, s, rs, zb, ag,
    load_sem, out_sem, send_sem, recv_sem,
):
    dp, vocab = lax.axis_index("dp"), lax.axis_index("vocab")
    y, c, x, z = dp // 2, lax.rem(dp, 2), vocab // Z, lax.rem(vocab, Z)
    mine = y * X + x
    columns = g.shape[1]
    half = columns // 2
    tiles = half // LANES

    def device(y, c, x, z):
        return (y * 2 + c, x * Z + z)

    sibling = device(y, 1 - c, x, z)
    y_peers = [device(lax.rem(y + k, Y), c, x, z) for k in range(1, Y)]
    x_peers = [device(y, c, lax.rem(x + k, X), z) for k in range(1, X)]
    z_peers = [device(y, c, x, lax.rem(z + k, Z)) for k in range(1, Z)]
    places = [lax.rem(mine + k, PLANE) for k in range(1, PLANE)]
    plane_peers = [device(p // X, c, lax.rem(p, X), z) for p in places]

    loads = []
    for k in range(columns // STEP):
        part = pl.ds(k * STEP, STEP)
        loads.append([
            pltpu.make_async_copy(hbm.at[:, part], vmem.at[:, part], load_sem.at[n, k])
            for n, (hbm, vmem) in enumerate(((g_hbm, g), (e_hbm, e)))
        ])
        for copy in loads[-1]:
            copy.start()

    barrier = pltpu.get_barrier_semaphore()
    everyone = [sibling] + plane_peers + z_peers
    for peer in everyone:
        pl.semaphore_signal(barrier, inc=1, device_id=peer, device_id_type=MESH)

    sent = []

    def send(src, dst, peers, phase):
        sources = src if isinstance(src, list) else [src] * len(peers)
        for source, peer in zip(sources, peers):
            pltpu.make_async_remote_copy(
                src_ref=source, dst_ref=dst, send_sem=send_sem.at[phase], recv_sem=recv_sem.at[phase],
                device_id=peer, device_id_type=MESH,
            ).start()

    def arrive(whole, phase):
        pltpu.make_async_copy(whole, whole, recv_sem.at[phase]).wait()
        sent.append((whole, phase))

    def columns_of(which, k):
        return pl.ds(pl.multiple_of(which * half + k * STEP, LANES), STEP)

    def gathered(it, which, k):
        parts = []
        for column in range(k * STEP // LANES, (k + 1) * STEP // LANES):
            rows = []
            for r in range(4):
                tile = column * 4 + r
                pair, at = tile // 9, tile % 9
                place, at = (2 * pair, at) if at < WINDOW else (2 * pair + 1, at - WINDOW + 1)
                rows.append(ag[it, which, place, at])
            parts.append(jnp.concatenate(rows, axis=0))
        return jnp.concatenate(parts, axis=1)

    def left_part(total, q, where):
        q3 = jnp.concatenate(split(q), axis=0)
        return total + (dot(g[:, where], q3, 1, 1) + dot(e[:, where], q3, 1, 1))

    def right_half(it, l3, which):
        for k in range(half // STEP):
            where = columns_of(which, k)
            part = dot(l3, g[:, where], 1, 0) + dot(l3, e[:, where], 1, 0)
            part = part[:RANK] + part[RANK : 2 * RANK] + part[2 * RANK :]
            for n in range(STEP // LANES):
                tile = (k * STEP // LANES + n) * 4
                u[it, which, tile : tile + 4] = part[:, n * LANES : (n + 1) * LANES].reshape(4, 8, LANES)

    total = jnp.zeros((g.shape[0], 3 * RANK), F32)
    inverse = None
    for it in range(ITERS):
        base = 8 * it
        if it == 0:
            for k in range(columns // STEP):
                for copy in loads[k]:
                    copy.wait()
                where = pl.ds(k * STEP, STEP)
                total = left_part(total, q_ref[:, where], where)
            pl.semaphore_wait(barrier, len(everyone))
        else:
            total = jnp.zeros_like(total)
            for k in range(half // STEP):
                total = left_part(total, gathered(it - 1, c, k), columns_of(c, k))
            arrive(ag.at[it - 1, 1 - c], base - 1)
            for k in range(half // STEP):
                total = left_part(total, gathered(it - 1, 1 - c, k), columns_of(1 - c, k))
        turned = jnp.concatenate([total, jnp.zeros((g.shape[0], LANES - 3 * RANK), F32)], axis=1).T
        lp[it] = turned[:RANK] + turned[RANK : 2 * RANK] + turned[2 * RANK : 3 * RANK]
        send(lp.at[it], lr.at[it], [sibling], base)
        arrive(lr.at[it], base)
        ly[it, y] = lp[it] + lr[it]
        send(ly.at[it, y], ly.at[it, y], y_peers, base + 1)
        arrive(ly.at[it, pl.ds(0, Y - 1)], base + 1)
        left = ly[it, 0] + ly[it, 1] + ly[it, 2] + ly[it, 3]
        if it > 0:
            left = dot(six(inverse * 0.125), six_rows(left), 1, 0)

        high, middle, low = split(left)
        other = jnp.concatenate([high, middle, low, high, middle, high], axis=1)
        square = dot(
            jnp.concatenate([high, high, high, middle, middle, low], axis=1),
            jnp.concatenate([other] * 4, axis=0), 1, 1,
        )
        lane = lax.broadcasted_iota(jnp.int32, (8, LANES), 1) // RANK
        packed = square[0:8]
        for r in range(1, 4):
            packed = jnp.where(lane == r, square[8 * r : 8 * r + 8], packed)
        gx[it, x] = packed
        send(gx.at[it, x], gx.at[it, x], x_peers, base + 2)

        l3 = jnp.concatenate([high, middle, low], axis=0)
        right_half(it, l3, 1 - c)
        send(u.at[it, 1 - c], pr.at[it], [sibling], base + 3)
        right_half(it, l3, c)
        arrive(pr.at[it], base + 3)
        s[it] = u[it, c] + pr[it]
        send([s.at[it, pl.ds(9 * p // 2, WINDOW)] for p in places], rs.at[it, mine], plane_peers, base + 4)
        rs[it, mine] = s[it, pl.ds(9 * mine // 2, WINDOW)]
        arrive(gx.at[it, pl.ds(0, X - 1)], base + 2)
        zb[it, z, WINDOW] = gx[it, 0] + gx[it, 1] + gx[it, 2] + gx[it, 3]
        arrive(rs.at[it, pl.ds(0, PLANE - 1)], base + 4)
        piece = rs[it, 0]
        for p in range(1, PLANE):
            piece = piece + rs[it, p]
        zb[it, z, 0:WINDOW] = piece
        send(zb.at[it, z], zb.at[it, z], z_peers, base + 5)
        arrive(zb.at[it, pl.ds(0, Z - 1)], base + 5)
        piece = zb[it, 0]
        for p in range(1, Z):
            piece = piece + zb[it, p]
        ag[it, c, mine] = piece[:WINDOW]
        send(ag.at[it, c, mine], ag.at[it, c, mine], plane_peers, base + 6)
        inverse = lower_inverse(piece[WINDOW])
        arrive(ag.at[it, c, pl.ds(0, PLANE - 1)], base + 6)
        send(ag.at[it, c], ag.at[it, c], [sibling], base + 7)

    last = ITERS - 1
    inverse6 = six(inverse)
    high, middle, _ = split(dot(inverse6, six_rows(left), 1, 0))
    basis3 = jnp.concatenate([high, high, middle], axis=0).astype(F32).T.astype(BF16)
    inverse6 = (inverse6.astype(F32) * 0.125).astype(BF16)
    outs = []
    for which in (c, 1 - c):
        if len(outs) > 0:
            arrive(ag.at[last, 1 - c], 8 * last + 7)
        for k in range(half // STEP):
            where = columns_of(which, k)
            right = dot(inverse6, six_rows(gathered(last, which, k)), 1, 0)
            rf[:, where] = right
            high, middle, _ = split(right)
            approx = dot(basis3, jnp.concatenate([high, middle, high], axis=0), 1, 0)
            o[:, where] = (g[:, where].astype(F32) + e[:, where].astype(F32) - approx).astype(BF16)
            n = len(outs)
            outs.append((
                pltpu.make_async_copy(o.at[:, where], o_hbm.at[:, where], out_sem.at[0, n]),
                pltpu.make_async_copy(rf.at[:, where], rf_hbm.at[:, where], out_sem.at[1, n]),
            ))
            for copy in outs[-1]:
                copy.start()
    for whole, phase in sent:
        pltpu.make_async_copy(whole, whole, send_sem.at[phase]).wait()
    for copies in outs:
        for copy in copies:
            copy.wait()


def body(grads, errors, start_q):
    g, e = grads[0], errors[0]
    rows, columns = g.shape
    tiles = columns // 2 // LANES * 4
    steps = columns // STEP
    hbm, vmem = pl.BlockSpec(memory_space=pl.ANY), pl.BlockSpec(memory_space=pltpu.VMEM)
    right, fresh = pl.pallas_call(
        kernel,
        out_shape=(jax.ShapeDtypeStruct((RANK, columns), F32), jax.ShapeDtypeStruct((rows, columns), BF16)),
        in_specs=[hbm, hbm, vmem],
        out_specs=(hbm, hbm),
        scratch_shapes=[
            pltpu.VMEM((rows, columns), BF16),
            pltpu.VMEM((rows, columns), BF16),
            pltpu.VMEM((rows, columns), BF16),
            pltpu.VMEM((RANK, columns), F32),
            pltpu.VMEM((ITERS, RANK, rows), F32),
            pltpu.VMEM((ITERS, RANK, rows), F32),
            pltpu.VMEM((ITERS, Y, RANK, rows), F32),
            pltpu.VMEM((ITERS, X, 8, LANES), F32),
            pltpu.VMEM((ITERS, 2, tiles, 8, LANES), F32),
            pltpu.VMEM((ITERS, tiles, 8, LANES), F32),
            pltpu.VMEM((ITERS, tiles, 8, LANES), F32),
            pltpu.VMEM((ITERS, PLANE, WINDOW, 8, LANES), F32),
            pltpu.VMEM((ITERS, Z, WINDOW + 1, 8, LANES), F32),
            pltpu.VMEM((ITERS, 2, PLANE, WINDOW, 8, LANES), F32),
            pltpu.SemaphoreType.DMA((2, steps)),
            pltpu.SemaphoreType.DMA((2, steps)),
            pltpu.SemaphoreType.DMA((8 * ITERS,)),
            pltpu.SemaphoreType.DMA((8 * ITERS,)),
        ],
        name="power_iterations",
        compiler_params=pltpu.CompilerParams(collective_id=0, has_side_effects=True, vmem_limit_bytes=48 << 20),
        cost_estimate=pl.CostEstimate(flops=5 * 2 * rows * columns * RANK, bytes_accessed=6 * rows * columns, transcendentals=0),
    )(g, e, start_q.T)
    return right.T, fresh[None]


def solution(mesh):
    return jax.shard_map(
        body,
        mesh=mesh,
        in_specs=(P("dp", "vocab", None), P("dp", "vocab", None), P()),
        out_specs=(P(), P("dp", "vocab", None)),
        check_vma=False,
    )
```

time: 882 us -> 82.5 us (0.09)
  waiting for transfers between devices: 542 us -> 0 us
  blocking collectives: 278 us -> 0 us
  Pallas kernels: 0 us -> 76.7 us
  matrix products: 31.9 us -> 0 us
  other arithmetic: 14.5 us -> 0 us
  between operations: 14.1 us -> 0.65 us
    psum x2 -> x0, waiting for transfers between devices: 542 us -> none  [body(): lax.psum(jnp.dot(mixed.T, basis, precision=hi), ('dp', 'vocab')) / replicas]
    psum x4 -> x0, blocking collectives: 278 us -> none  [the longest x2 231 us: body(): gram = lax.psum(jnp.dot(left.T, left, precision=hi), 'vocab')]
    pallas_call x0 -> x1, Pallas kernels: none -> 76.7 us  [body(): pl.pallas_call(kernel, out_shape=(jax.ShapeDtypeStruct((RANK, columns), F...]
    dot_general x7 -> x0, matrix products: 31.4 us -> none  [the longest x2 12.6 us: body(): left = lax.psum(jnp.dot(mixed, q_now, precision=hi), 'dp')]
    another operation x10 -> x0, other arithmetic: 13.4 us -> none  [the longest x6 7.19 us: body(): lower = jnp.linalg.cholesky(gram)]
  transfers between devices with their start and end apart: 2 -> 0, of which waited for: 2 -> 0; matrix products, arithmetic and copies ran while one was open for 0% -> 0% of each run, Pallas kernels for 0% -> 0%
where the time goes in v1:
time: 82.5 us; the launch traced here: 82.3 us
  Pallas kernels  76.7 us (93%)
  local copies, waits for them, and re-layouts  4.94 us (6%)
    pallas_call x1, Pallas kernels, body(): pl.pallas_call(kernel, out_shape=(jax.ShapeDtypeStruct((RANK, columns), F...  76.7 us
    unnamed x6, local copies, waits for them, and re-layouts  4.94 us

profile of v1, /device:TPU:1, one launch (start us, length us, event | category | flops | bytes accessed | tf_op | source)
XLA Modules:
  0.0 82.3 jit_solution(8532158282740954967)
XLA Ops:
  0.6 0.0 copy-start
  0.6 1.7 %copy-done = bf16[1,256,4608]{2,1,0:T(8,128)(2,1)S(1)} copy-done((bf16[1,256,4608]{2,1,0:T(8,128)(2,1)S(1)}, bf16[1,256,4608]{2,1,0:T(8,128)(2,1)}, u32[]{:S(2)}) %copy-start) | copy-done | bytes 2359320
  2.3 0.0 copy-start.1
  2.3 1.1 %copy-done.1 = f32[4608,32]{0,1:T(8,128)S(1)} copy-done((f32[4608,32]{0,1:T(8,128)S(1)}, f32[4608,32]{0,1:T(8,128)}, u32[]{:S(2)}) %copy-start.1) | copy-done | bytes 589848
  3.4 76.7 %power_iterations.1 = (f32[32,4608]{1,0:T(8,128)S(1)}, bf16[256,4608]{1,0:T(8,128)(2,1)S(1)}) custom-call(bf16[256,4608]{1,0:T(8,128)(2,1)S(1)} %bitcast.6, bf16[256,4608]{1,0:T(8,128)(2,1)} %bitcast.9, f32[32,4608]{1,0:T(8,128)S(1)} %bitcast.8), custom_call_target="tpu_custom_call" | custom-call | flops 377487360 | bytes 7077888 | tf_op jit(solution)/shard_map/power_iterations/pallas_call | solution.py:240
  80.1 0.8 copy.7
  80.9 1.4 %copy.8 = bf16[1,256,4608]{2,1,0:T(8,128)(2,1)} copy(bf16[1,256,4608]{2,1,0:T(8,128)(2,1)S(1)} %bitcast.5) | data formatting | bytes 4718592
Async XLA Ops:
  0.6 1.7 %copy-start = (bf16[1,256,4608]{2,1,0:T(8,128)(2,1)S(1)}, bf16[1,256,4608]{2,1,0:T(8,128)(2,1)}, u32[]{:S(2)}) copy-start(bf16[1,256,4608]{2,1,0:T(8,128)(2,1)} %param.3) | copy-start | bytes 7077892
  2.3 1.1 %copy-start.1 = (f32[4608,32]{0,1:T(8,128)S(1)}, f32[4608,32]{0,1:T(8,128)}, u32[]{:S(2)}) copy-start(f32[4608,32]{0,1:T(8,128)} %param.5) | copy-start | bytes 1769476

commit v2 on v1

v2 whole, which is shorter than its diff:
```python
import functools

import jax
import jax.numpy as jnp
from jax import lax
from jax.experimental import pallas as pl
from jax.experimental.pallas import tpu as pltpu
from jax.sharding import PartitionSpec as P

MESH = pl.DeviceIdType.MESH
F32, BF16 = jnp.float32, jnp.bfloat16
ITERS = 2
RANK = 32
LANES = 128
STEP = 768
WINDOW = 5
Y, X, Z = 4, 4, 8
PLANE = Y * X


def split(value):
    high = value.astype(BF16)
    rest = value - high.astype(F32)
    middle = rest.astype(BF16)
    return high, middle, (rest - middle.astype(F32)).astype(BF16)


def dot(a, b, over_a, over_b):
    return lax.dot_general(a, b, (((over_a,), (over_b,)), ((), ())), preferred_element_type=F32)


def lower_inverse(packed):
    row = lax.broadcasted_iota(jnp.int32, (RANK, LANES), 0)
    lane = lax.broadcasted_iota(jnp.int32, (RANK, LANES), 1)
    turned = [packed if r == 1 else pltpu.roll(packed, (RANK - RANK * r) % LANES, 1) for r in range(4)]
    work = jnp.where(lane < RANK, jnp.where(lane == row, 1.0, 0.0), jnp.concatenate(turned, axis=0))
    rows = row[:, :1]
    pivots = jnp.ones((RANK, 1), F32)
    for j in range(RANK):
        column, pivot = work[:, RANK + j : RANK + j + 1], work[j : j + 1, RANK + j : RANK + j + 1]
        factor = jnp.where(rows > j, column / pivot, 0.0)
        pivots = jnp.where(rows == j, pivot, pivots)
        work = work - factor * work[j : j + 1, :]
    return (work * lax.rsqrt(pivots))[:, :RANK]


def six(value):
    high, middle, low = split(value)
    return jnp.concatenate([high, high, high, middle, middle, low], axis=1)


def six_rows(value):
    high, middle, low = split(value)
    return jnp.concatenate([high, middle, low, high, middle, high], axis=0)


def gathered(windows, k):
    parts = []
    for column in range(k * STEP // LANES, (k + 1) * STEP // LANES):
        rows = []
        for r in range(4):
            tile = column * 4 + r
            pair, at = tile // 9, tile % 9
            place, at = (2 * pair, at) if at < WINDOW else (2 * pair + 1, at - WINDOW + 1)
            rows.append(windows[place, at])
        parts.append(jnp.concatenate(rows, axis=0))
    return jnp.concatenate(parts, axis=1)


def finish(windows, k, where, inverse6, basis3, g, e, rf, o):
    right = dot(inverse6, six_rows(gathered(windows, k)), 1, 0)
    rf[:, where] = right
    high, middle, _ = split(right)
    approx = dot(basis3, jnp.concatenate([high, middle, high], axis=0), 1, 0)
    o[:, where] = (g[:, where].astype(F32) + e[:, where].astype(F32) - approx).astype(BF16)


def columns_of(which, k, half):
    return pl.ds(pl.multiple_of(which * half + k * STEP, LANES), STEP)


def last_kernel(rf_in, o_in, g, e, windows, inverse6, basis3, rf_hbm, o_hbm, rf, o, sems):
    c = lax.rem(lax.axis_index("dp"), 2)
    half = g.shape[1] // 2
    copies = []

    def write(src, dst, where):
        copies.append(pltpu.make_async_copy(src.at[:, where], dst.at[:, where], sems.at[len(copies)]))
        copies[-1].start()

    for k in range(half // STEP):
        write(o_in, o_hbm, columns_of(c, k, half))
        write(rf_in, rf_hbm, columns_of(c, k, half))
    for k in range(half // STEP):
        where = columns_of(1 - c, k, half)
        finish(windows, k, where, inverse6[...], basis3[...], g, e, rf, o)
        write(o, o_hbm, where)
        write(rf, rf_hbm, where)
    for copy in copies:
        copy.wait()


def kernel(
    g_hbm, e_hbm, q_hbm, rf, o, g, e, back, inverse_ref, basis_ref,
    q, lp, lr, ly, gx, u, pr, s, rs, zb, ag,
    load_sem, send_sem, recv_sem,
):
    dp, vocab = lax.axis_index("dp"), lax.axis_index("vocab")
    y, c, x, z = dp // 2, lax.rem(dp, 2), vocab // Z, lax.rem(vocab, Z)
    mine = y * X + x
    columns = g.shape[1]
    half = columns // 2
    tiles = half // LANES

    def device(y, c, x, z):
        return (y * 2 + c, x * Z + z)

    sibling = device(y, 1 - c, x, z)
    y_peers = [device(lax.rem(y + k, Y), c, x, z) for k in range(1, Y)]
    x_peers = [device(y, c, lax.rem(x + k, X), z) for k in range(1, X)]
    z_peers = [device(y, c, x, lax.rem(z + k, Z)) for k in range(1, Z)]
    places = [lax.rem(mine + k, PLANE) for k in range(1, PLANE)]
    plane_peers = [device(p // X, c, lax.rem(p, X), z) for p in places]

    loads = []
    for k in range(columns // STEP):
        part = pl.ds(k * STEP, STEP)
        loads.append([
            pltpu.make_async_copy(hbm.at[:, part], vmem.at[:, part], load_sem.at[n, k])
            for n, (hbm, vmem) in enumerate(((q_hbm, q), (g_hbm, g), (e_hbm, e)))
        ])
        for copy in loads[-1]:
            copy.start()

    barrier = pltpu.get_barrier_semaphore()
    everyone = [sibling] + plane_peers + z_peers
    for peer in everyone:
        pl.semaphore_signal(barrier, inc=1, device_id=peer, device_id_type=MESH)

    sent = []

    pending = {}

    def send(src, dst, peers, phase, whole):
        pending[phase] = whole
        sources = src if isinstance(src, list) else [src] * len(peers)
        for source, peer in zip(sources, peers):
            pltpu.make_async_remote_copy(
                src_ref=source, dst_ref=dst, send_sem=send_sem.at[phase], recv_sem=recv_sem.at[phase],
                device_id=peer, device_id_type=MESH,
            ).start()

    def arrive(phase):
        whole = pending.pop(phase)
        pltpu.make_async_copy(whole, whole, recv_sem.at[phase]).wait()
        sent.append((whole, phase))

    def left_part(total, q, where):
        q3 = jnp.concatenate(split(q), axis=0)
        return total + (dot(g[:, where], q3, 1, 1) + dot(e[:, where], q3, 1, 1))

    def right_half(it, l3, which):
        for k in range(half // STEP):
            where = columns_of(which, k, half)
            part = dot(l3, g[:, where], 1, 0) + dot(l3, e[:, where], 1, 0)
            part = part[:RANK] + part[RANK : 2 * RANK] + part[2 * RANK :]
            for n in range(STEP // LANES):
                tile = (k * STEP // LANES + n) * 4
                u[it, which, tile : tile + 4] = part[:, n * LANES : (n + 1) * LANES].reshape(4, 8, LANES)

    total = jnp.zeros((g.shape[0], 3 * RANK), F32)
    inverse = None
    for it in range(ITERS):
        base = 8 * it
        if it == 0:
            for k in range(columns // STEP):
                for copy in loads[k]:
                    copy.wait()
                where = pl.ds(k * STEP, STEP)
                total = left_part(total, q[:, where], where)
            pl.semaphore_wait(barrier, len(everyone))
        else:
            total = jnp.zeros_like(total)
            for k in range(half // STEP):
                total = left_part(total, gathered(ag.at[it - 1], k), columns_of(c, k, half))
            arrive(base - 1)
            for k in range(half // STEP):
                total = left_part(total, gathered(back, k), columns_of(1 - c, k, half))
        turned = jnp.concatenate([total, jnp.zeros((g.shape[0], LANES - 3 * RANK), F32)], axis=1).T
        lp[it] = turned[:RANK] + turned[RANK : 2 * RANK] + turned[2 * RANK : 3 * RANK]
        send(lp.at[it], lr.at[it], [sibling], base, lr.at[it])
        arrive(base)
        ly[it, y] = lp[it] + lr[it]
        send(ly.at[it, y], ly.at[it, y], y_peers, base + 1, ly.at[it, pl.ds(0, Y - 1)])
        arrive(base + 1)
        left = ly[it, 0] + ly[it, 1] + ly[it, 2] + ly[it, 3]
        if it > 0:
            left = dot(six(inverse * 0.125), six_rows(left), 1, 0)

        high, middle, low = split(left)
        other = jnp.concatenate([high, middle, low, high, middle, high], axis=1)
        square = dot(
            jnp.concatenate([high, high, high, middle, middle, low], axis=1),
            jnp.concatenate([other] * 4, axis=0), 1, 1,
        )
        lane = lax.broadcasted_iota(jnp.int32, (8, LANES), 1) // RANK
        packed = square[0:8]
        for r in range(1, 4):
            packed = jnp.where(lane == r, square[8 * r : 8 * r + 8], packed)
        gx[it, x] = packed
        send(gx.at[it, x], gx.at[it, x], x_peers, base + 2, gx.at[it, pl.ds(0, X - 1)])

        l3 = jnp.concatenate([high, middle, low], axis=0)
        right_half(it, l3, 1 - c)
        send(u.at[it, 1 - c], pr.at[it], [sibling], base + 3, pr.at[it])
        right_half(it, l3, c)
        arrive(base + 3)
        s[it] = u[it, c] + pr[it]
        send([s.at[it, pl.ds(9 * p // 2, WINDOW)] for p in places], rs.at[it, mine], plane_peers, base + 4, rs.at[it, pl.ds(0, PLANE - 1)])
        rs[it, mine] = s[it, pl.ds(9 * mine // 2, WINDOW)]
        arrive(base + 2)
        zb[it, z, WINDOW] = gx[it, 0] + gx[it, 1] + gx[it, 2] + gx[it, 3]
        arrive(base + 4)
        piece = rs[it, 0]
        for p in range(1, PLANE):
            piece = piece + rs[it, p]
        zb[it, z, 0:WINDOW] = piece
        send(zb.at[it, z], zb.at[it, z], z_peers, base + 5, zb.at[it, pl.ds(0, Z - 1)])
        arrive(base + 5)
        piece = zb[it, 0]
        for p in range(1, Z):
            piece = piece + zb[it, p]
        ag[it, mine] = piece[:WINDOW]
        send(ag.at[it, mine], ag.at[it, mine], plane_peers, base + 6, ag.at[it, pl.ds(0, PLANE - 1)])
        inverse = lower_inverse(piece[WINDOW])
        arrive(base + 6)
        send(ag.at[it], back, [sibling], base + 7, back)

    last = ITERS - 1
    inverse6 = six(inverse)
    high, middle, _ = split(dot(inverse6, six_rows(left), 1, 0))
    basis3 = jnp.concatenate([high, high, middle], axis=0).astype(F32).T.astype(BF16)
    inverse6 = (inverse6.astype(F32) * 0.125).astype(BF16)
    inverse_ref[...] = inverse6
    basis_ref[...] = basis3
    for k in range(half // STEP):
        finish(ag.at[last], k, columns_of(c, k, half), inverse6, basis3, g, e, rf, o)
    arrive(8 * last + 7)
    for whole, phase in sent:
        pltpu.make_async_copy(whole, whole, send_sem.at[phase]).wait()


def body(grads, errors, start_q):
    g, e = grads[0], errors[0]
    rows, columns = g.shape
    tiles = columns // 2 // LANES * 4
    steps = columns // STEP
    hbm, vmem = pl.BlockSpec(memory_space=pltpu.HBM), pl.BlockSpec(memory_space=pltpu.VMEM)
    held = pl.pallas_call(
        kernel,
        out_shape=(
            pltpu.VMEM((RANK, columns), F32),
            pltpu.VMEM((rows, columns), BF16),
            pltpu.VMEM((rows, columns), BF16),
            pltpu.VMEM((rows, columns), BF16),
            pltpu.VMEM((PLANE, WINDOW, 8, LANES), F32),
            pltpu.VMEM((RANK, 6 * RANK), BF16),
            pltpu.VMEM((rows, 3 * RANK), BF16),
        ),
        in_specs=[hbm] * 3,
        out_specs=(vmem,) * 7,
        scratch_shapes=[
            pltpu.VMEM((RANK, columns), F32),
            pltpu.VMEM((ITERS, RANK, rows), F32),
            pltpu.VMEM((ITERS, RANK, rows), F32),
            pltpu.VMEM((ITERS, Y, RANK, rows), F32),
            pltpu.VMEM((ITERS, X, 8, LANES), F32),
            pltpu.VMEM((ITERS, 2, tiles, 8, LANES), F32),
            pltpu.VMEM((ITERS, tiles, 8, LANES), F32),
            pltpu.VMEM((ITERS, tiles, 8, LANES), F32),
            pltpu.VMEM((ITERS, PLANE, WINDOW, 8, LANES), F32),
            pltpu.VMEM((ITERS, Z, WINDOW + 1, 8, LANES), F32),
            pltpu.VMEM((ITERS, PLANE, WINDOW, 8, LANES), F32),
            pltpu.SemaphoreType.DMA((3, steps)),
            pltpu.SemaphoreType.DMA((8 * ITERS,)),
            pltpu.SemaphoreType.DMA((8 * ITERS,)),
        ],
        name="power_iterations",
        compiler_params=pltpu.CompilerParams(collective_id=0, has_side_effects=True, vmem_limit_bytes=50 << 20),
        cost_estimate=pl.CostEstimate(flops=5 * 2 * rows * columns * RANK, bytes_accessed=6 * rows * columns, transcendentals=0),
    )(g, e, start_q.T)
    right, fresh = pl.pallas_call(
        last_kernel,
        out_shape=(jax.ShapeDtypeStruct((RANK, columns), F32), jax.ShapeDtypeStruct((rows, columns), BF16)),
        in_specs=[vmem] * 7,
        out_specs=(hbm, hbm),
        scratch_shapes=[
            pltpu.VMEM((RANK, columns), F32),
            pltpu.VMEM((rows, columns), BF16),
            pltpu.SemaphoreType.DMA((2 * steps,)),
        ],
        name="other_half",
        compiler_params=pltpu.CompilerParams(vmem_limit_bytes=16 << 20),
        cost_estimate=pl.CostEstimate(flops=2 * rows * columns * RANK, bytes_accessed=3 * rows * columns, transcendentals=0),
    )(*held)
    return right.T, fresh[None]


def solution(mesh):
    return jax.shard_map(
        body,
        mesh=mesh,
        in_specs=(P("dp", "vocab", None), P("dp", "vocab", None), P()),
        out_specs=(P(), P("dp", "vocab", None)),
        check_vma=False,
    )
```

time: 82.5 us -> 78.1 us (0.947)
  local copies, waits for them, and re-layouts: 4.94 us -> 0 us
    unnamed x6 -> x0, local copies, waits for them, and re-layouts: 4.94 us -> none
    pallas_call x1 -> x2, Pallas kernels: 76.7 us -> 77.4 us  [the longest x1 75.6 us: body(): pl.pallas_call(kernel, out_shape=(pltpu.VMEM((RANK, columns), F32), pltpu...]
where the time goes in v2:
time: 78.1 us; the launch traced here: 78 us
  Pallas kernels  77.4 us (99%)
    pallas_call x1, Pallas kernels, body(): pl.pallas_call(kernel, out_shape=(pltpu.VMEM((RANK, columns), F32), pltpu...  75.6 us
    pallas_call x1, Pallas kernels, body(): pl.pallas_call(last_kernel, out_shape=(jax.ShapeDtypeStruct((RANK, column...  1.8 us

profile of v2, /device:TPU:1, one launch (start us, length us, event | category | flops | bytes accessed | tf_op | source)
XLA Modules:
  0.0 78.0 jit_solution(928049206104257533)
XLA Ops:
  0.6 75.6 %power_iterations.1 = (f32[32,4608]{1,0:T(8,128)S(1)}, bf16[256,4608]{1,0:T(8,128)(2,1)S(1)}, bf16[256,4608]{1,0:T(8,128)(2,1)S(1)}, bf16[256,4608]{1,0:T(8,128)...) custom-call(bf16[256,4608]{1,0:T(8,128)(2,1)} %bitcast.5, ...), custom_call_target="tpu_custom_call" | custom-call | flops 377487360 | bytes 7077888 | tf_op jit(solution)/shard_map/power_iterations/pallas_call | solution.py:259
  76.2 1.8 %other_half.1 = (f32[32,4608]{1,0:T(8,128)}, bf16[256,4608]{1,0:T(8,128)(2,1)}) custom-call(f32[32,4608]{1,0:T(8,128)S(1)} %get-tuple-element.11.rf_in, bf16[256,4608]{1,0:T(8,128)(2,1)S(1)} %get-tuple-element.12.o_in, bf16[256,4608]{1,0:T(8,128)(2,1)S(1)} %get-tuple-element.13.g, bf16[256,4608]{1,0:T(8,128)(2,1)S(1)} %get-tuple-element.14.e, ...), custom_call_target="tpu_custom_call" | custom-call | flops 75497472 | bytes 3538944 | tf_op jit(solution)/shard_map/other_half/pallas_call | solution.py:292

commit v3 on v2

--- a/solution.py
+++ b/solution.py
@@ -16,6 +16,7 @@
 WINDOW = 5
 Y, X, Z = 4, 4, 8
 PLANE = Y * X
+PHASES = 9
 
 
 def split(value):
@@ -102,7 +103,7 @@
 
 def kernel(
     g_hbm, e_hbm, q_hbm, rf, o, g, e, back, inverse_ref, basis_ref,
-    q, lp, lr, ly, gx, u, pr, s, rs, zb, ag,
+    q, lp, lr, ly, gx, gz, u, pr, s, rs, zb, ag,
     load_sem, send_sem, recv_sem,
 ):
     dp, vocab = lax.axis_index("dp"), lax.axis_index("vocab")
@@ -116,11 +117,15 @@
         return (y * 2 + c, x * Z + z)
 
     sibling = device(y, 1 - c, x, z)
-    y_peers = [device(lax.rem(y + k, Y), c, x, z) for k in range(1, Y)]
-    x_peers = [device(y, c, lax.rem(x + k, X), z) for k in range(1, X)]
-    z_peers = [device(y, c, x, lax.rem(z + k, Z)) for k in range(1, Z)]
-    places = [lax.rem(mine + k, PLANE) for k in range(1, PLANE)]
-    plane_peers = [device(p // X, c, lax.rem(p, X), z) for p in places]
+    y_peers = [device(lax.rem(y + k, Y), c, x, z) for k in (2, 1, 3)]
+    x_peers = [device(y, c, lax.rem(x + k, X), z) for k in (2, 1, 3)]
+    far = lambda k, size: min(k, size - k)
+    z_peers = [device(y, c, x, lax.rem(z + k, Z)) for k in sorted(range(1, Z), key=lambda k: -far(k, Z))]
+    steps = [(j, k) for j in range(Y) for k in range(X) if j + k > 0]
+    steps.sort(key=lambda jk: -far(jk[0], Y) - far(jk[1], X))
+    across = [(lax.rem(y + j, Y), lax.rem(x + k, X)) for j, k in steps]
+    places = [j * X + k for j, k in across]
+    plane_peers = [device(j, c, k, z) for j, k in across]
 
     loads = []
     for k in range(columns // STEP):
@@ -159,7 +164,7 @@
         q3 = jnp.concatenate(split(q), axis=0)
         return total + (dot(g[:, where], q3, 1, 1) + dot(e[:, where], q3, 1, 1))
 
-    def right_half(it, l3, which):
+    def right_half(it, l3, which, send_it):
         for k in range(half // STEP):
             where = columns_of(which, k, half)
             part = dot(l3, g[:, where], 1, 0) + dot(l3, e[:, where], 1, 0)
@@ -167,11 +172,14 @@
             for n in range(STEP // LANES):
                 tile = (k * STEP // LANES + n) * 4
                 u[it, which, tile : tile + 4] = part[:, n * LANES : (n + 1) * LANES].reshape(4, 8, LANES)
+            if send_it:
+                span = pl.ds(k * STEP // LANES * 4, STEP // LANES * 4)
+                send(u.at[it, which, span], pr.at[it, span], [sibling], PHASES * it + 3, pr.at[it])
 
     total = jnp.zeros((g.shape[0], 3 * RANK), F32)
     inverse = None
     for it in range(ITERS):
-        base = 8 * it
+        base = PHASES * it
         if it == 0:
             for k in range(columns // STEP):
                 for copy in loads[k]:
@@ -183,7 +191,7 @@
             total = jnp.zeros_like(total)
             for k in range(half // STEP):
                 total = left_part(total, gathered(ag.at[it - 1], k), columns_of(c, k, half))
-            arrive(base - 1)
+            arrive(base - PHASES + 7)
             for k in range(half // STEP):
                 total = left_part(total, gathered(back, k), columns_of(1 - c, k, half))
         turned = jnp.concatenate([total, jnp.zeros((g.shape[0], LANES - 3 * RANK), F32)], axis=1).T
@@ -198,6 +206,9 @@
             left = dot(six(inverse * 0.125), six_rows(left), 1, 0)
 
         high, middle, low = split(left)
+        l3 = jnp.concatenate([high, middle, low], axis=0)
+        right_half(it, l3, 1 - c, True)
+
         other = jnp.concatenate([high, middle, low, high, middle, high], axis=1)
         square = dot(
             jnp.concatenate([high, high, high, middle, middle, low], axis=1),
@@ -210,29 +221,32 @@
         gx[it, x] = packed
         send(gx.at[it, x], gx.at[it, x], x_peers, base + 2, gx.at[it, pl.ds(0, X - 1)])
 
-        l3 = jnp.concatenate([high, middle, low], axis=0)
-        right_half(it, l3, 1 - c)
-        send(u.at[it, 1 - c], pr.at[it], [sibling], base + 3, pr.at[it])
-        right_half(it, l3, c)
+        right_half(it, l3, c, False)
         arrive(base + 3)
+
         s[it] = u[it, c] + pr[it]
         send([s.at[it, pl.ds(9 * p // 2, WINDOW)] for p in places], rs.at[it, mine], plane_peers, base + 4, rs.at[it, pl.ds(0, PLANE - 1)])
         rs[it, mine] = s[it, pl.ds(9 * mine // 2, WINDOW)]
         arrive(base + 2)
-        zb[it, z, WINDOW] = gx[it, 0] + gx[it, 1] + gx[it, 2] + gx[it, 3]
+        gz[it, z] = gx[it, 0] + gx[it, 1] + gx[it, 2] + gx[it, 3]
+        send(gz.at[it, z], gz.at[it, z], z_peers, base + 8, gz.at[it, pl.ds(0, Z - 1)])
         arrive(base + 4)
         piece = rs[it, 0]
         for p in range(1, PLANE):
             piece = piece + rs[it, p]
-        zb[it, z, 0:WINDOW] = piece
+        zb[it, z] = piece
         send(zb.at[it, z], zb.at[it, z], z_peers, base + 5, zb.at[it, pl.ds(0, Z - 1)])
+        arrive(base + 8)
+        gram = gz[it, 0]
+        for p in range(1, Z):
+            gram = gram + gz[it, p]
+        inverse = lower_inverse(gram)
         arrive(base + 5)
         piece = zb[it, 0]
         for p in range(1, Z):
             piece = piece + zb[it, p]
-        ag[it, mine] = piece[:WINDOW]
+        ag[it, mine] = piece
         send(ag.at[it, mine], ag.at[it, mine], plane_peers, base + 6, ag.at[it, pl.ds(0, PLANE - 1)])
-        inverse = lower_inverse(piece[WINDOW])
         arrive(base + 6)
         send(ag.at[it], back, [sibling], base + 7, back)
 
@@ -245,7 +259,7 @@
     basis_ref[...] = basis3
     for k in range(half // STEP):
         finish(ag.at[last], k, columns_of(c, k, half), inverse6, basis3, g, e, rf, o)
-    arrive(8 * last + 7)
+    arrive(PHASES * last + 7)
     for whole, phase in sent:
         pltpu.make_async_copy(whole, whole, send_sem.at[phase]).wait()
 
@@ -275,15 +289,16 @@
             pltpu.VMEM((ITERS, RANK, rows), F32),
             pltpu.VMEM((ITERS, Y, RANK, rows), F32),
             pltpu.VMEM((ITERS, X, 8, LANES), F32),
+            pltpu.VMEM((ITERS, Z, 8, LANES), F32),
             pltpu.VMEM((ITERS, 2, tiles, 8, LANES), F32),
             pltpu.VMEM((ITERS, tiles, 8, LANES), F32),
             pltpu.VMEM((ITERS, tiles, 8, LANES), F32),
             pltpu.VMEM((ITERS, PLANE, WINDOW, 8, LANES), F32),
-            pltpu.VMEM((ITERS, Z, WINDOW + 1, 8, LANES), F32),
+            pltpu.VMEM((ITERS, Z, WINDOW, 8, LANES), F32),
             pltpu.VMEM((ITERS, PLANE, WINDOW, 8, LANES), F32),
             pltpu.SemaphoreType.DMA((3, steps)),
-            pltpu.SemaphoreType.DMA((8 * ITERS,)),
-            pltpu.SemaphoreType.DMA((8 * ITERS,)),
+            pltpu.SemaphoreType.DMA((PHASES * ITERS,)),
+            pltpu.SemaphoreType.DMA((PHASES * ITERS,)),
         ],
         name="power_iterations",
         compiler_params=pltpu.CompilerParams(collective_id=0, has_side_effects=True, vmem_limit_bytes=50 << 20),

time: 78.1 us -> 68.9 us (0.88)
  Pallas kernels: 77.4 us -> 68.2 us
    pallas_call x1, Pallas kernels: 75.6 us -> 66.4 us  [body(): pl.pallas_call(kernel, out_shape=(pltpu.VMEM((RANK, columns), F32), pltpu...]
where the time goes in v3:
time: 68.9 us
  Pallas kernels  68.2 us (99%)
    pallas_call x1, Pallas kernels, body(): pl.pallas_call(kernel, out_shape=(pltpu.VMEM((RANK, columns), F32), pltpu...  66.4 us
    pallas_call x1, Pallas kernels, body(): pl.pallas_call(last_kernel, out_shape=(jax.ShapeDtypeStruct((RANK, column...  1.8 us

profile of v3, /device:TPU:1, one launch (start us, length us, event | category | flops | bytes accessed | tf_op | source)
XLA Modules:
  0.0 68.9 jit_solution(12745653975529491478)
XLA Ops:
  0.6 66.4 %power_iterations.1 = (f32[32,4608]{1,0:T(8,128)S(1)}, bf16[256,4608]{1,0:T(8,128)(2,1)S(1)}, bf16[256,4608]{1,0:T(8,128)(2,1)S(1)}, bf16[256,4608]{1,0:T(8,128)...) custom-call(bf16[256,4608]{1,0:T(8,128)(2,1)} %bitcast.5, ...), custom_call_target="tpu_custom_call" | custom-call | flops 377487360 | bytes 7077888 | tf_op jit(solution)/shard_map/power_iterations/pallas_call | solution.py:273
  67.1 1.8 %other_half.1 = (f32[32,4608]{1,0:T(8,128)}, bf16[256,4608]{1,0:T(8,128)(2,1)}) custom-call(f32[32,4608]{1,0:T(8,128)S(1)} %get-tuple-element.11.rf_in, bf16[256,4608]{1,0:T(8,128)(2,1)S(1)} %get-tuple-element.12.o_in, bf16[256,4608]{1,0:T(8,128)(2,1)S(1)} %get-tuple-element.13.g, bf16[256,4608]{1,0:T(8,128)(2,1)S(1)} %get-tuple-element.14.e, ...), custom_call_target="tpu_custom_call" | custom-call | flops 75497472 | bytes 3538944 | tf_op jit(solution)/shard_map/other_half/pallas_call | solution.py:307

commit v4 on v3

--- a/solution.py
+++ b/solution.py
@@ -17,6 +17,7 @@
 Y, X, Z = 4, 4, 8
 PLANE = Y * X
 PHASES = 9
+BULK = PHASES * ITERS
 
 
 def split(value):
@@ -103,7 +104,7 @@
 
 def kernel(
     g_hbm, e_hbm, q_hbm, rf, o, g, e, back, inverse_ref, basis_ref,
-    q, lp, lr, ly, gx, gz, u, pr, s, rs, zb, ag,
+    q, lp, lr, ly, gx, gz, s, rs, zb, ag, mixed, mixed_in, m3,
     load_sem, send_sem, recv_sem,
 ):
     dp, vocab = lax.axis_index("dp"), lax.axis_index("vocab")
@@ -127,12 +128,12 @@
     places = [j * X + k for j, k in across]
     plane_peers = [device(j, c, k, z) for j, k in across]
 
+    chunks = [(which, k, columns_of(which, k, half)) for which in (1 - c, c) for k in range(half // STEP)]
     loads = []
-    for k in range(columns // STEP):
-        part = pl.ds(k * STEP, STEP)
+    for n, (which, k, part) in enumerate(chunks):
         loads.append([
-            pltpu.make_async_copy(hbm.at[:, part], vmem.at[:, part], load_sem.at[n, k])
-            for n, (hbm, vmem) in enumerate(((q_hbm, q), (g_hbm, g), (e_hbm, e)))
+            pltpu.make_async_copy(hbm.at[:, part], vmem.at[:, part], load_sem.at[m, n])
+            for m, (hbm, vmem) in enumerate(((q_hbm, q), (g_hbm, g), (e_hbm, e)))
         ])
         for copy in loads[-1]:
             copy.start()
@@ -160,54 +161,59 @@
         pltpu.make_async_copy(whole, whole, recv_sem.at[phase]).wait()
         sent.append((whole, phase))
 
-    def left_part(total, q, where):
-        q3 = jnp.concatenate(split(q), axis=0)
-        return total + (dot(g[:, where], q3, 1, 1) + dot(e[:, where], q3, 1, 1))
-
-    def right_half(it, l3, which, send_it):
-        for k in range(half // STEP):
-            where = columns_of(which, k, half)
-            part = dot(l3, g[:, where], 1, 0) + dot(l3, e[:, where], 1, 0)
-            part = part[:RANK] + part[RANK : 2 * RANK] + part[2 * RANK :]
-            for n in range(STEP // LANES):
-                tile = (k * STEP // LANES + n) * 4
-                u[it, which, tile : tile + 4] = part[:, n * LANES : (n + 1) * LANES].reshape(4, 8, LANES)
-            if send_it:
-                span = pl.ds(k * STEP // LANES * 4, STEP // LANES * 4)
-                send(u.at[it, which, span], pr.at[it, span], [sibling], PHASES * it + 3, pr.at[it])
-
-    total = jnp.zeros((g.shape[0], 3 * RANK), F32)
+    def split3(q):
+        return jnp.concatenate(split(q), axis=0)
+
+    size = g.shape[0]
     inverse = None
     for it in range(ITERS):
         base = PHASES * it
+        total = jnp.zeros((size, 3 * RANK), F32)
         if it == 0:
-            for k in range(columns // STEP):
-                for copy in loads[k]:
+            for copies, (which, k, where) in zip(loads, chunks):
+                for copy in copies:
                     copy.wait()
-                where = pl.ds(k * STEP, STEP)
-                total = left_part(total, q[:, where], where)
+                q3 = split3(q[:, where])
+                total = total + (dot(g[:, where], q3, 1, 1) + dot(e[:, where], q3, 1, 1))
             pl.semaphore_wait(barrier, len(everyone))
         else:
-            total = jnp.zeros_like(total)
             for k in range(half // STEP):
-                total = left_part(total, gathered(ag.at[it - 1], k), columns_of(c, k, half))
-            arrive(base - PHASES + 7)
-            for k in range(half // STEP):
-                total = left_part(total, gathered(back, k), columns_of(1 - c, k, half))
-        turned = jnp.concatenate([total, jnp.zeros((g.shape[0], LANES - 3 * RANK), F32)], axis=1).T
+                part = dot(m3[:, k * STEP : (k + 1) * STEP], split3(gathered(ag.at[it - 1], k)), 1, 1)
+                total = total + (part[:size] + part[size : 2 * size] + part[2 * size :])
+        turned = jnp.concatenate([total, jnp.zeros((size, LANES - 3 * RANK), F32)], axis=1).T
         lp[it] = turned[:RANK] + turned[RANK : 2 * RANK] + turned[2 * RANK : 3 * RANK]
         send(lp.at[it], lr.at[it], [sibling], base, lr.at[it])
+        if it == 0:
+            for k in range(half // STEP):
+                where = columns_of(1 - c, k, half)
+                mixed[k] = g[:, where].astype(F32) + e[:, where].astype(F32)
         arrive(base)
         ly[it, y] = lp[it] + lr[it]
         send(ly.at[it, y], ly.at[it, y], y_peers, base + 1, ly.at[it, pl.ds(0, Y - 1)])
+        if it == 0:
+            for k in range(half // STEP):
+                send(mixed.at[k], mixed_in.at[k], [sibling], BULK + k, mixed_in.at[k])
+        if it == 0:
+            for k in range(half // STEP):
+                where = columns_of(c, k, half)
+                here = g[:, where].astype(F32) + e[:, where].astype(F32)
+                arrive(BULK + k)
+                for n, part in enumerate(split(here + mixed_in[k])):
+                    m3[n * size : (n + 1) * size, k * STEP : (k + 1) * STEP] = part
         arrive(base + 1)
         left = ly[it, 0] + ly[it, 1] + ly[it, 2] + ly[it, 3]
         if it > 0:
             left = dot(six(inverse * 0.125), six_rows(left), 1, 0)
 
         high, middle, low = split(left)
-        l3 = jnp.concatenate([high, middle, low], axis=0)
-        right_half(it, l3, 1 - c, True)
+        l9 = jnp.concatenate([jnp.concatenate([high, middle, low], axis=0)] * 3, axis=1)
+        for k in range(half // STEP):
+            part = dot(l9, m3[:, k * STEP : (k + 1) * STEP], 1, 0)
+            part = part[:RANK] + part[RANK : 2 * RANK] + part[2 * RANK :]
+            for n in range(STEP // LANES):
+                tile = (k * STEP // LANES + n) * 4
+                s[it, tile : tile + 4] = part[:, n * LANES : (n + 1) * LANES].reshape(4, 8, LANES)
+        send([s.at[it, pl.ds(9 * p // 2, WINDOW)] for p in places], rs.at[it, mine], plane_peers, base + 4, rs.at[it, pl.ds(0, PLANE - 1)])
 
         other = jnp.concatenate([high, middle, low, high, middle, high], axis=1)
         square = dot(
@@ -221,34 +227,29 @@
         gx[it, x] = packed
         send(gx.at[it, x], gx.at[it, x], x_peers, base + 2, gx.at[it, pl.ds(0, X - 1)])
 
-        right_half(it, l3, c, False)
-        arrive(base + 3)
-
-        s[it] = u[it, c] + pr[it]
-        send([s.at[it, pl.ds(9 * p // 2, WINDOW)] for p in places], rs.at[it, mine], plane_peers, base + 4, rs.at[it, pl.ds(0, PLANE - 1)])
         rs[it, mine] = s[it, pl.ds(9 * mine // 2, WINDOW)]
-        arrive(base + 2)
-        gz[it, z] = gx[it, 0] + gx[it, 1] + gx[it, 2] + gx[it, 3]
-        send(gz.at[it, z], gz.at[it, z], z_peers, base + 8, gz.at[it, pl.ds(0, Z - 1)])
         arrive(base + 4)
         piece = rs[it, 0]
         for p in range(1, PLANE):
             piece = piece + rs[it, p]
         zb[it, z] = piece
         send(zb.at[it, z], zb.at[it, z], z_peers, base + 5, zb.at[it, pl.ds(0, Z - 1)])
-        arrive(base + 8)
-        gram = gz[it, 0]
-        for p in range(1, Z):
-            gram = gram + gz[it, p]
-        inverse = lower_inverse(gram)
+        arrive(base + 2)
+        gz[it, z] = gx[it, 0] + gx[it, 1] + gx[it, 2] + gx[it, 3]
+        send(gz.at[it, z], gz.at[it, z], z_peers, base + 8, gz.at[it, pl.ds(0, Z - 1)])
         arrive(base + 5)
         piece = zb[it, 0]
         for p in range(1, Z):
             piece = piece + zb[it, p]
         ag[it, mine] = piece
         send(ag.at[it, mine], ag.at[it, mine], plane_peers, base + 6, ag.at[it, pl.ds(0, PLANE - 1)])
+        arrive(base + 8)
+        gram = gz[it, 0]
+        for p in range(1, Z):
+            gram = gram + gz[it, p]
+        inverse = lower_inverse(gram)
         arrive(base + 6)
-        send(ag.at[it], back, [sibling], base + 7, back)
+    send(ag.at[ITERS - 1], back, [sibling], PHASES * ITERS - 2, back)
 
     last = ITERS - 1
     inverse6 = six(inverse)
@@ -259,7 +260,7 @@
     basis_ref[...] = basis3
     for k in range(half // STEP):
         finish(ag.at[last], k, columns_of(c, k, half), inverse6, basis3, g, e, rf, o)
-    arrive(PHASES * last + 7)
+    arrive(PHASES * ITERS - 2)
     for whole, phase in sent:
         pltpu.make_async_copy(whole, whole, send_sem.at[phase]).wait()
 
@@ -290,15 +291,16 @@
             pltpu.VMEM((ITERS, Y, RANK, rows), F32),
             pltpu.VMEM((ITERS, X, 8, LANES), F32),
             pltpu.VMEM((ITERS, Z, 8, LANES), F32),
-            pltpu.VMEM((ITERS, 2, tiles, 8, LANES), F32),
-            pltpu.VMEM((ITERS, tiles, 8, LANES), F32),
             pltpu.VMEM((ITERS, tiles, 8, LANES), F32),
             pltpu.VMEM((ITERS, PLANE, WINDOW, 8, LANES), F32),
             pltpu.VMEM((ITERS, Z, WINDOW, 8, LANES), F32),
             pltpu.VMEM((ITERS, PLANE, WINDOW, 8, LANES), F32),
+            pltpu.VMEM((steps // 2, rows, STEP), F32),
+            pltpu.VMEM((steps // 2, rows, STEP), F32),
+            pltpu.VMEM((3 * rows, columns // 2), BF16),
             pltpu.SemaphoreType.DMA((3, steps)),
-            pltpu.SemaphoreType.DMA((PHASES * ITERS,)),
-            pltpu.SemaphoreType.DMA((PHASES * ITERS,)),
+            pltpu.SemaphoreType.DMA((PHASES * ITERS + steps // 2,)),
+            pltpu.SemaphoreType.DMA((PHASES * ITERS + steps // 2,)),
         ],
         name="power_iterations",
         compiler_params=pltpu.CompilerParams(collective_id=0, has_side_effects=True, vmem_limit_bytes=50 << 20),

time: 68.9 us -> 65.8 us (0.955)
  Pallas kernels: 68.2 us -> 65.1 us
    pallas_call x1, Pallas kernels: 66.4 us -> 63.3 us  [body(): pl.pallas_call(kernel, out_shape=(pltpu.VMEM((RANK, columns), F32), pltpu...]
where the time goes in v4:
time: 65.8 us; the launch traced here: 65.7 us
  Pallas kernels  65.1 us (99%)
    pallas_call x1, Pallas kernels, body(): pl.pallas_call(kernel, out_shape=(pltpu.VMEM((RANK, columns), F32), pltpu...  63.3 us
    pallas_call x1, Pallas kernels, body(): pl.pallas_call(last_kernel, out_shape=(jax.ShapeDtypeStruct((RANK, column...  1.8 us

profile of v4, /device:TPU:1, one launch (start us, length us, event | category | flops | bytes accessed | tf_op | source)
XLA Modules:
  0.0 65.7 jit_solution(2323863913121694673)
XLA Ops:
  0.6 63.3 %power_iterations.1 = (f32[32,4608]{1,0:T(8,128)S(1)}, bf16[256,4608]{1,0:T(8,128)(2,1)S(1)}, bf16[256,4608]{1,0:T(8,128)(2,1)S(1)}, bf16[256,4608]{1,0:T(8,128)...) custom-call(bf16[256,4608]{1,0:T(8,128)(2,1)} %bitcast.5, ...), custom_call_target="tpu_custom_call" | custom-call | flops 377487360 | bytes 7077888 | tf_op jit(solution)/shard_map/power_iterations/pallas_call | solution.py:274
  63.9 1.8 %other_half.1 = (f32[32,4608]{1,0:T(8,128)}, bf16[256,4608]{1,0:T(8,128)(2,1)}) custom-call(f32[32,4608]{1,0:T(8,128)S(1)} %get-tuple-element.11.rf_in, bf16[256,4608]{1,0:T(8,128)(2,1)S(1)} %get-tuple-element.12.o_in, bf16[256,4608]{1,0:T(8,128)(2,1)S(1)} %get-tuple-element.13.g, bf16[256,4608]{1,0:T(8,128)(2,1)S(1)} %get-tuple-element.14.e, ...), custom_call_target="tpu_custom_call" | custom-call | flops 75497472 | bytes 3538944 | tf_op jit(solution)/shard_map/other_half/pallas_call | solution.py:309

commit v5 on v4

--- a/solution.py
+++ b/solution.py
@@ -16,7 +16,8 @@
 WINDOW = 5
 Y, X, Z = 4, 4, 8
 PLANE = Y * X
-PHASES = 9
+PARTS = (2, 2, 1)
+PHASES = 15
 BULK = PHASES * ITERS
 
 
@@ -187,12 +188,10 @@
             for k in range(half // STEP):
                 where = columns_of(1 - c, k, half)
                 mixed[k] = g[:, where].astype(F32) + e[:, where].astype(F32)
+                send(mixed.at[k], mixed_in.at[k], [sibling], BULK + k, mixed_in.at[k])
         arrive(base)
         ly[it, y] = lp[it] + lr[it]
         send(ly.at[it, y], ly.at[it, y], y_peers, base + 1, ly.at[it, pl.ds(0, Y - 1)])
-        if it == 0:
-            for k in range(half // STEP):
-                send(mixed.at[k], mixed_in.at[k], [sibling], BULK + k, mixed_in.at[k])
         if it == 0:
             for k in range(half // STEP):
                 where = columns_of(c, k, half)
@@ -213,7 +212,15 @@
             for n in range(STEP // LANES):
                 tile = (k * STEP // LANES + n) * 4
                 s[it, tile : tile + 4] = part[:, n * LANES : (n + 1) * LANES].reshape(4, 8, LANES)
-        send([s.at[it, pl.ds(9 * p // 2, WINDOW)] for p in places], rs.at[it, mine], plane_peers, base + 4, rs.at[it, pl.ds(0, PLANE - 1)])
+        spans, at = [], 0
+        for n, size_of in enumerate(PARTS):
+            spans.append((6 + 3 * n, pl.ds(at, size_of), at, size_of))
+            at = at + size_of
+        for phase, span, at, size_of in spans:
+            send(
+                [s.at[it, pl.ds(9 * p // 2 + at, size_of)] for p in places], rs.at[it, mine, span],
+                plane_peers, base + phase, rs.at[it, pl.ds(0, PLANE - 1), span],
+            )
 
         other = jnp.concatenate([high, middle, low, high, middle, high], axis=1)
         square = dot(
@@ -228,28 +235,31 @@
         send(gx.at[it, x], gx.at[it, x], x_peers, base + 2, gx.at[it, pl.ds(0, X - 1)])
 
         rs[it, mine] = s[it, pl.ds(9 * mine // 2, WINDOW)]
-        arrive(base + 4)
-        piece = rs[it, 0]
-        for p in range(1, PLANE):
-            piece = piece + rs[it, p]
-        zb[it, z] = piece
-        send(zb.at[it, z], zb.at[it, z], z_peers, base + 5, zb.at[it, pl.ds(0, Z - 1)])
+        for phase, span, at, size_of in spans:
+            arrive(base + phase)
+            piece = rs[it, 0, span]
+            for p in range(1, PLANE):
+                piece = piece + rs[it, p, span]
+            zb[it, z, span] = piece
+            send(zb.at[it, z, span], zb.at[it, z, span], z_peers, base + phase + 1, zb.at[it, pl.ds(0, Z - 1), span])
         arrive(base + 2)
         gz[it, z] = gx[it, 0] + gx[it, 1] + gx[it, 2] + gx[it, 3]
-        send(gz.at[it, z], gz.at[it, z], z_peers, base + 8, gz.at[it, pl.ds(0, Z - 1)])
-        arrive(base + 5)
-        piece = zb[it, 0]
-        for p in range(1, Z):
-            piece = piece + zb[it, p]
-        ag[it, mine] = piece
-        send(ag.at[it, mine], ag.at[it, mine], plane_peers, base + 6, ag.at[it, pl.ds(0, PLANE - 1)])
-        arrive(base + 8)
+        send(gz.at[it, z], gz.at[it, z], z_peers, base + 3, gz.at[it, pl.ds(0, Z - 1)])
+        for phase, span, at, size_of in spans:
+            arrive(base + phase + 1)
+            piece = zb[it, 0, span]
+            for p in range(1, Z):
+                piece = piece + zb[it, p, span]
+            ag[it, mine, span] = piece
+            send(ag.at[it, mine, span], ag.at[it, mine, span], plane_peers, base + phase + 2, ag.at[it, pl.ds(0, PLANE - 1), span])
+        arrive(base + 3)
         gram = gz[it, 0]
         for p in range(1, Z):
             gram = gram + gz[it, p]
         inverse = lower_inverse(gram)
-        arrive(base + 6)
-    send(ag.at[ITERS - 1], back, [sibling], PHASES * ITERS - 2, back)
+        for phase, span, at, size_of in spans:
+            arrive(base + phase + 2)
+    send(ag.at[ITERS - 1], back, [sibling], PHASES * ITERS - PHASES + 4, back)
 
     last = ITERS - 1
     inverse6 = six(inverse)
@@ -260,7 +270,7 @@
     basis_ref[...] = basis3
     for k in range(half // STEP):
         finish(ag.at[last], k, columns_of(c, k, half), inverse6, basis3, g, e, rf, o)
-    arrive(PHASES * ITERS - 2)
+    arrive(PHASES * ITERS - PHASES + 4)
     for whole, phase in sent:
         pltpu.make_async_copy(whole, whole, send_sem.at[phase]).wait()
 

time: 65.8 us -> 63 us (0.957)
  Pallas kernels: 65.1 us -> 62.3 us
    pallas_call x1, Pallas kernels: 63.3 us -> 60.5 us  [body(): pl.pallas_call(kernel, out_shape=(pltpu.VMEM((RANK, columns), F32), pltpu...]
where the time goes in v5:
time: 63 us; the launch traced here: 62.9 us
  Pallas kernels  62.3 us (99%)
  between operations  0.64 us (1%)
    pallas_call x1, Pallas kernels, body(): pl.pallas_call(kernel, out_shape=(pltpu.VMEM((RANK, columns), F32), pltpu...  60.5 us
    pallas_call x1, Pallas kernels, body(): pl.pallas_call(last_kernel, out_shape=(jax.ShapeDtypeStruct((RANK, column...  1.79 us

profile of v5, /device:TPU:1, one launch (start us, length us, event | category | flops | bytes accessed | tf_op | source)
XLA Modules:
  0.0 62.9 jit_solution(15355244838224787849)
XLA Ops:
  0.6 60.5 %power_iterations.1 = (f32[32,4608]{1,0:T(8,128)S(1)}, bf16[256,4608]{1,0:T(8,128)(2,1)S(1)}, bf16[256,4608]{1,0:T(8,128)(2,1)S(1)}, bf16[256,4608]{1,0:T(8,128)...) custom-call(bf16[256,4608]{1,0:T(8,128)(2,1)} %bitcast.5, ...), custom_call_target="tpu_custom_call" | custom-call | flops 377487360 | bytes 7077888 | tf_op jit(solution)/shard_map/power_iterations/pallas_call | solution.py:284
  61.1 1.8 %other_half.1 = (f32[32,4608]{1,0:T(8,128)}, bf16[256,4608]{1,0:T(8,128)(2,1)}) custom-call(f32[32,4608]{1,0:T(8,128)S(1)} %get-tuple-element.11.rf_in, bf16[256,4608]{1,0:T(8,128)(2,1)S(1)} %get-tuple-element.12.o_in, bf16[256,4608]{1,0:T(8,128)(2,1)S(1)} %get-tuple-element.13.g, bf16[256,4608]{1,0:T(8,128)(2,1)S(1)} %get-tuple-element.14.e, ...), custom_call_target="tpu_custom_call" | custom-call | flops 75497472 | bytes 3538944 | tf_op jit(solution)/shard_map/other_half/pallas_call | solution.py:319

commit v6 on v5

--- a/solution.py
+++ b/solution.py
@@ -13,10 +13,9 @@
 RANK = 32
 LANES = 128
 STEP = 768
-WINDOW = 5
+WINDOW = 2
 Y, X, Z = 4, 4, 8
 PLANE = Y * X
-PARTS = (2, 2, 1)
 PHASES = 15
 BULK = PHASES * ITERS
 
@@ -59,13 +58,11 @@
 
 def gathered(windows, k):
     parts = []
-    for column in range(k * STEP // LANES, (k + 1) * STEP // LANES):
+    for column in range(STEP // LANES):
         rows = []
         for r in range(4):
-            tile = column * 4 + r
-            pair, at = tile // 9, tile % 9
-            place, at = (2 * pair, at) if at < WINDOW else (2 * pair + 1, at - WINDOW + 1)
-            rows.append(windows[place, at])
+            pair, at = (column * 4 + r) // 3, (column * 4 + r) % 3
+            rows.append(windows[k, 2 * pair + at // WINDOW, at if at < WINDOW else WINDOW - 1])
         parts.append(jnp.concatenate(rows, axis=0))
     return jnp.concatenate(parts, axis=1)
 
@@ -179,6 +176,7 @@
             pl.semaphore_wait(barrier, len(everyone))
         else:
             for k in range(half // STEP):
+                arrive(base - PHASES + 8 + 3 * k)
                 part = dot(m3[:, k * STEP : (k + 1) * STEP], split3(gathered(ag.at[it - 1], k)), 1, 1)
                 total = total + (part[:size] + part[size : 2 * size] + part[2 * size :])
         turned = jnp.concatenate([total, jnp.zeros((size, LANES - 3 * RANK), F32)], axis=1).T
@@ -210,16 +208,10 @@
             part = dot(l9, m3[:, k * STEP : (k + 1) * STEP], 1, 0)
             part = part[:RANK] + part[RANK : 2 * RANK] + part[2 * RANK :]
             for n in range(STEP // LANES):
-                tile = (k * STEP // LANES + n) * 4
-                s[it, tile : tile + 4] = part[:, n * LANES : (n + 1) * LANES].reshape(4, 8, LANES)
-        spans, at = [], 0
-        for n, size_of in enumerate(PARTS):
-            spans.append((6 + 3 * n, pl.ds(at, size_of), at, size_of))
-            at = at + size_of
-        for phase, span, at, size_of in spans:
+                s[it, k, 4 * n : 4 * n + 4] = part[:, n * LANES : (n + 1) * LANES].reshape(4, 8, LANES)
             send(
-                [s.at[it, pl.ds(9 * p // 2 + at, size_of)] for p in places], rs.at[it, mine, span],
-                plane_peers, base + phase, rs.at[it, pl.ds(0, PLANE - 1), span],
+                [s.at[it, k, pl.ds(3 * p // 2, WINDOW)] for p in places], rs.at[it, k, mine],
+                plane_peers, base + 6 + 3 * k, rs.at[it, k, pl.ds(0, PLANE - 1)],
             )
 
         other = jnp.concatenate([high, middle, low, high, middle, high], axis=1)
@@ -234,32 +226,29 @@
         gx[it, x] = packed
         send(gx.at[it, x], gx.at[it, x], x_peers, base + 2, gx.at[it, pl.ds(0, X - 1)])
 
-        rs[it, mine] = s[it, pl.ds(9 * mine // 2, WINDOW)]
-        for phase, span, at, size_of in spans:
-            arrive(base + phase)
-            piece = rs[it, 0, span]
+        for k in range(half // STEP):
+            rs[it, k, mine] = s[it, k, pl.ds(3 * mine // 2, WINDOW)]
+            arrive(base + 6 + 3 * k)
+            piece = rs[it, k, 0]
             for p in range(1, PLANE):
-                piece = piece + rs[it, p, span]
-            zb[it, z, span] = piece
-            send(zb.at[it, z, span], zb.at[it, z, span], z_peers, base + phase + 1, zb.at[it, pl.ds(0, Z - 1), span])
+                piece = piece + rs[it, k, p]
+            zb[it, k, z] = piece
+            send(zb.at[it, k, z], zb.at[it, k, z], z_peers, base + 7 + 3 * k, zb.at[it, k, pl.ds(0, Z - 1)])
         arrive(base + 2)
         gz[it, z] = gx[it, 0] + gx[it, 1] + gx[it, 2] + gx[it, 3]
         send(gz.at[it, z], gz.at[it, z], z_peers, base + 3, gz.at[it, pl.ds(0, Z - 1)])
-        for phase, span, at, size_of in spans:
-            arrive(base + phase + 1)
-            piece = zb[it, 0, span]
+        for k in range(half // STEP):
+            arrive(base + 7 + 3 * k)
+            piece = zb[it, k, 0]
             for p in range(1, Z):
-                piece = piece + zb[it, p, span]
-            ag[it, mine, span] = piece
-            send(ag.at[it, mine, span], ag.at[it, mine, span], plane_peers, base + phase + 2, ag.at[it, pl.ds(0, PLANE - 1), span])
+                piece = piece + zb[it, k, p]
+            ag[it, k, mine] = piece
+            send(ag.at[it, k, mine], ag.at[it, k, mine], plane_peers, base + 8 + 3 * k, ag.at[it, k, pl.ds(0, PLANE - 1)])
         arrive(base + 3)
         gram = gz[it, 0]
         for p in range(1, Z):
             gram = gram + gz[it, p]
         inverse = lower_inverse(gram)
-        for phase, span, at, size_of in spans:
-            arrive(base + phase + 2)
-    send(ag.at[ITERS - 1], back, [sibling], PHASES * ITERS - PHASES + 4, back)
 
     last = ITERS - 1
     inverse6 = six(inverse)
@@ -269,8 +258,10 @@
     inverse_ref[...] = inverse6
     basis_ref[...] = basis3
     for k in range(half // STEP):
+        arrive(PHASES * last + 8 + 3 * k)
+        send(ag.at[last, k], back.at[k], [sibling], PHASES * last + 4, back)
         finish(ag.at[last], k, columns_of(c, k, half), inverse6, basis3, g, e, rf, o)
-    arrive(PHASES * ITERS - PHASES + 4)
+    arrive(PHASES * last + 4)
     for whole, phase in sent:
         pltpu.make_async_copy(whole, whole, send_sem.at[phase]).wait()
 
@@ -278,7 +269,6 @@
 def body(grads, errors, start_q):
     g, e = grads[0], errors[0]
     rows, columns = g.shape
-    tiles = columns // 2 // LANES * 4
     steps = columns // STEP
     hbm, vmem = pl.BlockSpec(memory_space=pltpu.HBM), pl.BlockSpec(memory_space=pltpu.VMEM)
     held = pl.pallas_call(
@@ -288,7 +278,7 @@
             pltpu.VMEM((rows, columns), BF16),
             pltpu.VMEM((rows, columns), BF16),
             pltpu.VMEM((rows, columns), BF16),
-            pltpu.VMEM((PLANE, WINDOW, 8, LANES), F32),
+            pltpu.VMEM((steps // 2, PLANE, WINDOW, 8, LANES), F32),
             pltpu.VMEM((RANK, 6 * RANK), BF16),
             pltpu.VMEM((rows, 3 * RANK), BF16),
         ),
@@ -301,10 +291,10 @@
             pltpu.VMEM((ITERS, Y, RANK, rows), F32),
             pltpu.VMEM((ITERS, X, 8, LANES), F32),
             pltpu.VMEM((ITERS, Z, 8, LANES), F32),
-            pltpu.VMEM((ITERS, tiles, 8, LANES), F32),
-            pltpu.VMEM((ITERS, PLANE, WINDOW, 8, LANES), F32),
-            pltpu.VMEM((ITERS, Z, WINDOW, 8, LANES), F32),
-            pltpu.VMEM((ITERS, PLANE, WINDOW, 8, LANES), F32),
+            pltpu.VMEM((ITERS, steps // 2, STEP // LANES * 4, 8, LANES), F32),
+            pltpu.VMEM((ITERS, steps // 2, PLANE, WINDOW, 8, LANES), F32),
+            pltpu.VMEM((ITERS, steps // 2, Z, WINDOW, 8, LANES), F32),
+            pltpu.VMEM((ITERS, steps // 2, PLANE, WINDOW, 8, LANES), F32),
             pltpu.VMEM((steps // 2, rows, STEP), F32),
             pltpu.VMEM((steps // 2, rows, STEP), F32),
             pltpu.VMEM((3 * rows, columns // 2), BF16),

time: 63 us -> 61.9 us (0.983)
  Pallas kernels: 62.3 us -> 61.2 us
    pallas_call x1, Pallas kernels: 60.5 us -> 59.4 us  [body(): pl.pallas_call(kernel, out_shape=(pltpu.VMEM((RANK, columns), F32), pltpu...]
where the time goes in v6:
time: 61.9 us; the launch traced here: 61.8 us
  Pallas kernels  61.2 us (99%)
  between operations  0.64 us (1%)
    pallas_call x1, Pallas kernels, body(): pl.pallas_call(kernel, out_shape=(pltpu.VMEM((RANK, columns), F32), pltpu...  59.4 us
    pallas_call x1, Pallas kernels, body(): pl.pallas_call(last_kernel, out_shape=(jax.ShapeDtypeStruct((RANK, column...  1.8 us

profile of v6, /device:TPU:1, one launch (start us, length us, event | category | flops | bytes accessed | tf_op | source)
XLA Modules:
  0.0 61.8 jit_solution(1099735821626328520)
XLA Ops:
  0.6 59.4 %power_iterations.1 = (f32[32,4608]{1,0:T(8,128)S(1)}, bf16[256,4608]{1,0:T(8,128)(2,1)S(1)}, bf16[256,4608]{1,0:T(8,128)(2,1)S(1)}, bf16[256,4608]{1,0:T(8,128)...) custom-call(bf16[256,4608]{1,0:T(8,128)(2,1)} %bitcast.5, ...), custom_call_target="tpu_custom_call" | custom-call | flops 377487360 | bytes 7077888 | tf_op jit(solution)/shard_map/power_iterations/pallas_call | solution.py:274
  60.0 1.8 %other_half.1 = (f32[32,4608]{1,0:T(8,128)}, bf16[256,4608]{1,0:T(8,128)(2,1)}) custom-call(f32[32,4608]{1,0:T(8,128)S(1)} %get-tuple-element.11.rf_in, bf16[256,4608]{1,0:T(8,128)(2,1)S(1)} %get-tuple-element.12.o_in, bf16[256,4608]{1,0:T(8,128)(2,1)S(1)} %get-tuple-element.13.g, bf16[256,4608]{1,0:T(8,128)(2,1)S(1)} %get-tuple-element.14.e, ...), custom_call_target="tpu_custom_call" | custom-call | flops 75497472 | bytes 3538944 | tf_op jit(solution)/shard_map/other_half/pallas_call | solution.py:309

commit v7 on v6

--- a/solution.py
+++ b/solution.py
@@ -13,10 +13,11 @@
 RANK = 32
 LANES = 128
 STEP = 768
-WINDOW = 2
+PARTS = ((0, 1024, 2), (1024, 768, 2), (1792, 512, 1))
+TILES = tuple(width // 32 for _, width, _ in PARTS)
 Y, X, Z = 4, 4, 8
 PLANE = Y * X
-PHASES = 15
+PHASES = 16
 BULK = PHASES * ITERS
 
 
@@ -58,11 +59,11 @@
 
 def gathered(windows, k):
     parts = []
-    for column in range(STEP // LANES):
+    for column in range(TILES[k] // 4):
         rows = []
-        for r in range(4):
-            pair, at = (column * 4 + r) // 3, (column * 4 + r) % 3
-            rows.append(windows[k, 2 * pair + at // WINDOW, at if at < WINDOW else WINDOW - 1])
+        for tile in range(4 * column, 4 * column + 4):
+            place = next(p for p in range(PLANE) if tile - p * TILES[k] // PLANE < PARTS[k][2])
+            rows.append(windows[k, place, tile - place * TILES[k] // PLANE])
         parts.append(jnp.concatenate(rows, axis=0))
     return jnp.concatenate(parts, axis=1)
 
@@ -79,6 +80,10 @@
     return pl.ds(pl.multiple_of(which * half + k * STEP, LANES), STEP)
 
 
+def part_of(which, k, half):
+    return pl.ds(pl.multiple_of(which * half + PARTS[k][0], LANES), PARTS[k][1])
+
+
 def last_kernel(rf_in, o_in, g, e, windows, inverse6, basis3, rf_hbm, o_hbm, rf, o, sems):
     c = lax.rem(lax.axis_index("dp"), 2)
     half = g.shape[1] // 2
@@ -88,11 +93,11 @@
         copies.append(pltpu.make_async_copy(src.at[:, where], dst.at[:, where], sems.at[len(copies)]))
         copies[-1].start()
 
-    for k in range(half // STEP):
-        write(o_in, o_hbm, columns_of(c, k, half))
-        write(rf_in, rf_hbm, columns_of(c, k, half))
-    for k in range(half // STEP):
-        where = columns_of(1 - c, k, half)
+    for k in range(len(PARTS)):
+        write(o_in, o_hbm, part_of(c, k, half))
+        write(rf_in, rf_hbm, part_of(c, k, half))
+    for k in range(len(PARTS)):
+        where = part_of(1 - c, k, half)
         finish(windows, k, where, inverse6[...], basis3[...], g, e, rf, o)
         write(o, o_hbm, where)
         write(rf, rf_hbm, where)
@@ -175,9 +180,9 @@
                 total = total + (dot(g[:, where], q3, 1, 1) + dot(e[:, where], q3, 1, 1))
             pl.semaphore_wait(barrier, len(everyone))
         else:
-            for k in range(half // STEP):
+            for k, (first, width, _) in enumerate(PARTS):
                 arrive(base - PHASES + 8 + 3 * k)
-                part = dot(m3[:, k * STEP : (k + 1) * STEP], split3(gathered(ag.at[it - 1], k)), 1, 1)
+                part = dot(m3[:, first : first + width], split3(gathered(ag.at[it - 1], k)), 1, 1)
                 total = total + (part[:size] + part[size : 2 * size] + part[2 * size :])
         turned = jnp.concatenate([total, jnp.zeros((size, LANES - 3 * RANK), F32)], axis=1).T
         lp[it] = turned[:RANK] + turned[RANK : 2 * RANK] + turned[2 * RANK : 3 * RANK]
@@ -204,14 +209,14 @@
 
         high, middle, low = split(left)
         l9 = jnp.concatenate([jnp.concatenate([high, middle, low], axis=0)] * 3, axis=1)
-        for k in range(half // STEP):
-            part = dot(l9, m3[:, k * STEP : (k + 1) * STEP], 1, 0)
+        for k, (first, width, window) in enumerate(PARTS):
+            part = dot(l9, m3[:, first : first + width], 1, 0)
             part = part[:RANK] + part[RANK : 2 * RANK] + part[2 * RANK :]
-            for n in range(STEP // LANES):
+            for n in range(width // LANES):
                 s[it, k, 4 * n : 4 * n + 4] = part[:, n * LANES : (n + 1) * LANES].reshape(4, 8, LANES)
             send(
-                [s.at[it, k, pl.ds(3 * p // 2, WINDOW)] for p in places], rs.at[it, k, mine],
-                plane_peers, base + 6 + 3 * k, rs.at[it, k, pl.ds(0, PLANE - 1)],
+                [s.at[it, k, pl.ds(p * TILES[k] // PLANE, window)] for p in places], rs.at[it, k, mine, pl.ds(0, window)],
+                plane_peers, base + 6 + 3 * k, rs.at[it, k, pl.ds(0, PLANE - 1), pl.ds(0, window)],
             )
 
         other = jnp.concatenate([high, middle, low, high, middle, high], axis=1)
@@ -226,24 +231,32 @@
         gx[it, x] = packed
         send(gx.at[it, x], gx.at[it, x], x_peers, base + 2, gx.at[it, pl.ds(0, X - 1)])
 
-        for k in range(half // STEP):
-            rs[it, k, mine] = s[it, k, pl.ds(3 * mine // 2, WINDOW)]
+        for k, (_, _, window) in enumerate(PARTS):
+            span = pl.ds(0, window)
+            rs[it, k, mine, span] = s[it, k, pl.ds(mine * TILES[k] // PLANE, window)]
             arrive(base + 6 + 3 * k)
-            piece = rs[it, k, 0]
+            piece = rs[it, k, 0, span]
             for p in range(1, PLANE):
-                piece = piece + rs[it, k, p]
-            zb[it, k, z] = piece
-            send(zb.at[it, k, z], zb.at[it, k, z], z_peers, base + 7 + 3 * k, zb.at[it, k, pl.ds(0, Z - 1)])
+                piece = piece + rs[it, k, p, span]
+            zb[it, k, z, span] = piece
+            send(
+                zb.at[it, k, z, span], zb.at[it, k, z, span],
+                z_peers, base + 7 + 3 * k, zb.at[it, k, pl.ds(0, Z - 1), span],
+            )
         arrive(base + 2)
         gz[it, z] = gx[it, 0] + gx[it, 1] + gx[it, 2] + gx[it, 3]
         send(gz.at[it, z], gz.at[it, z], z_peers, base + 3, gz.at[it, pl.ds(0, Z - 1)])
-        for k in range(half // STEP):
+        for k, (_, _, window) in enumerate(PARTS):
+            span = pl.ds(0, window)
             arrive(base + 7 + 3 * k)
-            piece = zb[it, k, 0]
+            piece = zb[it, k, 0, span]
             for p in range(1, Z):
-                piece = piece + zb[it, k, p]
-            ag[it, k, mine] = piece
-            send(ag.at[it, k, mine], ag.at[it, k, mine], plane_peers, base + 8 + 3 * k, ag.at[it, k, pl.ds(0, PLANE - 1)])
+                piece = piece + zb[it, k, p, span]
+            ag[it, k, mine, span] = piece
+            send(
+                ag.at[it, k, mine, span], ag.at[it, k, mine, span],
+                plane_peers, base + 8 + 3 * k, ag.at[it, k, pl.ds(0, PLANE - 1), span],
+            )
         arrive(base + 3)
         gram = gz[it, 0]
         for p in range(1, Z):
@@ -257,11 +270,13 @@
     inverse6 = (inverse6.astype(F32) * 0.125).astype(BF16)
     inverse_ref[...] = inverse6
     basis_ref[...] = basis3
-    for k in range(half // STEP):
+    for k, (_, _, window) in enumerate(PARTS):
+        span = pl.ds(0, window)
         arrive(PHASES * last + 8 + 3 * k)
-        send(ag.at[last, k], back.at[k], [sibling], PHASES * last + 4, back)
-        finish(ag.at[last], k, columns_of(c, k, half), inverse6, basis3, g, e, rf, o)
-    arrive(PHASES * last + 4)
+        send(ag.at[last, k, :, span], back.at[k, :, span], [sibling], (4, 5, 15)[k] + PHASES * last, back.at[k, :, span])
+        finish(ag.at[last], k, part_of(c, k, half), inverse6, basis3, g, e, rf, o)
+    for phase in (4, 5, 15):
+        arrive(PHASES * last + phase)
     for whole, phase in sent:
         pltpu.make_async_copy(whole, whole, send_sem.at[phase]).wait()
 
@@ -278,7 +293,7 @@
             pltpu.VMEM((rows, columns), BF16),
             pltpu.VMEM((rows, columns), BF16),
             pltpu.VMEM((rows, columns), BF16),
-            pltpu.VMEM((steps // 2, PLANE, WINDOW, 8, LANES), F32),
+            pltpu.VMEM((len(PARTS), PLANE, 2, 8, LANES), F32),
             pltpu.VMEM((RANK, 6 * RANK), BF16),
             pltpu.VMEM((rows, 3 * RANK), BF16),
         ),
@@ -291,10 +306,10 @@
             pltpu.VMEM((ITERS, Y, RANK, rows), F32),
             pltpu.VMEM((ITERS, X, 8, LANES), F32),
             pltpu.VMEM((ITERS, Z, 8, LANES), F32),
-            pltpu.VMEM((ITERS, steps // 2, STEP // LANES * 4, 8, LANES), F32),
-            pltpu.VMEM((ITERS, steps // 2, PLANE, WINDOW, 8, LANES), F32),
-            pltpu.VMEM((ITERS, steps // 2, Z, WINDOW, 8, LANES), F32),
-            pltpu.VMEM((ITERS, steps // 2, PLANE, WINDOW, 8, LANES), F32),
+            pltpu.VMEM((ITERS, len(PARTS), max(TILES), 8, LANES), F32),
+            pltpu.VMEM((ITERS, len(PARTS), PLANE, 2, 8, LANES), F32),
+            pltpu.VMEM((ITERS, len(PARTS), Z, 2, 8, LANES), F32),
+            pltpu.VMEM((ITERS, len(PARTS), PLANE, 2, 8, LANES), F32),
             pltpu.VMEM((steps // 2, rows, STEP), F32),
             pltpu.VMEM((steps // 2, rows, STEP), F32),
             pltpu.VMEM((3 * rows, columns // 2), BF16),

time: 61.9 us -> 60.8 us (0.982)
  Pallas kernels: 61.2 us -> 60.1 us
    pallas_call x1, Pallas kernels: 59.4 us -> 58.4 us  [body(): pl.pallas_call(kernel, out_shape=(pltpu.VMEM((RANK, columns), F32), pltpu...]
where the time goes in v7:
time: 60.8 us; the launch traced here: 60.7 us
  Pallas kernels  60.1 us (99%)
  between operations  0.64 us (1%)
    pallas_call x1, Pallas kernels, body(): pl.pallas_call(kernel, out_shape=(pltpu.VMEM((RANK, columns), F32), pltpu...  58.4 us
    pallas_call x1, Pallas kernels, body(): pl.pallas_call(last_kernel, out_shape=(jax.ShapeDtypeStruct((RANK, column...  1.72 us

profile of v7, /device:TPU:1, one launch (start us, length us, event | category | flops | bytes accessed | tf_op | source)
XLA Modules:
  0.0 60.7 jit_solution(7133837615236973447)
XLA Ops:
  0.6 58.4 %power_iterations.1 = (f32[32,4608]{1,0:T(8,128)S(1)}, bf16[256,4608]{1,0:T(8,128)(2,1)S(1)}, bf16[256,4608]{1,0:T(8,128)(2,1)S(1)}, bf16[256,4608]{1,0:T(8,128)...) custom-call(bf16[256,4608]{1,0:T(8,128)(2,1)} %bitcast.5, ...), custom_call_target="tpu_custom_call" | custom-call | flops 377487360 | bytes 7077888 | tf_op jit(solution)/shard_map/power_iterations/pallas_call | solution.py:289
  59.0 1.7 %other_half.1 = (f32[32,4608]{1,0:T(8,128)}, bf16[256,4608]{1,0:T(8,128)(2,1)}) custom-call(f32[32,4608]{1,0:T(8,128)S(1)} %get-tuple-element.11.rf_in, bf16[256,4608]{1,0:T(8,128)(2,1)S(1)} %get-tuple-element.12.o_in, bf16[256,4608]{1,0:T(8,128)(2,1)S(1)} %get-tuple-element.13.g, bf16[256,4608]{1,0:T(8,128)(2,1)S(1)} %get-tuple-element.14.e, ...), custom_call_target="tpu_custom_call" | custom-call | flops 75497472 | bytes 3538944 | tf_op jit(solution)/shard_map/other_half/pallas_call | solution.py:324

commit v8 on v7

--- a/solution.py
+++ b/solution.py
@@ -163,6 +163,11 @@
         whole = pending.pop(phase)
         pltpu.make_async_copy(whole, whole, recv_sem.at[phase]).wait()
         sent.append((whole, phase))
+
+    def drain():
+        while sent:
+            whole, phase = sent.pop()
+            pltpu.make_async_copy(whole, whole, send_sem.at[phase]).wait()
 
     def split3(q):
         return jnp.concatenate(split(q), axis=0)
@@ -246,6 +251,7 @@
         arrive(base + 2)
         gz[it, z] = gx[it, 0] + gx[it, 1] + gx[it, 2] + gx[it, 3]
         send(gz.at[it, z], gz.at[it, z], z_peers, base + 3, gz.at[it, pl.ds(0, Z - 1)])
+        drain()
         for k, (_, _, window) in enumerate(PARTS):
             span = pl.ds(0, window)
             arrive(base + 7 + 3 * k)
@@ -277,8 +283,7 @@
         finish(ag.at[last], k, part_of(c, k, half), inverse6, basis3, g, e, rf, o)
     for phase in (4, 5, 15):
         arrive(PHASES * last + phase)
-    for whole, phase in sent:
-        pltpu.make_async_copy(whole, whole, send_sem.at[phase]).wait()
+    drain()
 
 
 def body(grads, errors, start_q):

time: 60.8 us -> 60.8 us (level)
  no operation moved by 1% of the time
where the time goes in v8:
time: 60.8 us; the launch traced here: 60.7 us
  Pallas kernels  60.1 us (99%)
  between operations  0.64 us (1%)
    pallas_call x1, Pallas kernels, body(): pl.pallas_call(kernel, out_shape=(pltpu.VMEM((RANK, columns), F32), pltpu...  58.3 us
    pallas_call x1, Pallas kernels, body(): pl.pallas_call(last_kernel, out_shape=(jax.ShapeDtypeStruct((RANK, column...  1.72 us

profile of v8, /device:TPU:1, one launch (start us, length us, event | category | flops | bytes accessed | tf_op | source)
XLA Modules:
  0.0 60.7 jit_solution(6581169954847591395)
XLA Ops:
  0.6 58.3 %power_iterations.1 = (f32[32,4608]{1,0:T(8,128)S(1)}, bf16[256,4608]{1,0:T(8,128)(2,1)S(1)}, bf16[256,4608]{1,0:T(8,128)(2,1)S(1)}, bf16[256,4608]{1,0:T(8,128)...) custom-call(bf16[256,4608]{1,0:T(8,128)(2,1)} %bitcast.5, ...), custom_call_target="tpu_custom_call" | custom-call | flops 377487360 | bytes 7077888 | tf_op jit(solution)/shard_map/power_iterations/pallas_call | solution.py:294
  59.0 1.7 %other_half.1 = (f32[32,4608]{1,0:T(8,128)}, bf16[256,4608]{1,0:T(8,128)(2,1)}) custom-call(f32[32,4608]{1,0:T(8,128)S(1)} %get-tuple-element.11.rf_in, bf16[256,4608]{1,0:T(8,128)(2,1)S(1)} %get-tuple-element.12.o_in, bf16[256,4608]{1,0:T(8,128)(2,1)S(1)} %get-tuple-element.13.g, bf16[256,4608]{1,0:T(8,128)(2,1)S(1)} %get-tuple-element.14.e, ...), custom_call_target="tpu_custom_call" | custom-call | flops 75497472 | bytes 3538944 | tf_op jit(solution)/shard_map/other_half/pallas_call | solution.py:329
